TPU v7x, 512 devices: a whole 4x8x8 slice. The times are simulated.
512 devices in a mesh: rep: 16 (over x_lo, z), fsdp: 32 (over y, x_hi, core).
Axes of the slice: x: 4 (x_hi: 2, x_lo: 2; x = x_hi * 2 + x_lo), y: 8, z: 8, core: 2. Of those that a mesh axis runs over, the one named last changes fastest.
Arguments:
- hid_acts: bfloat16 [1, 98304, 448], P(None, ('rep', 'fsdp')), may hold values from -16 to 16
- out_cot: bfloat16 [1, 98304, 4608], P(None, ('rep', 'fsdp')), may hold values from -6 to 6
- momentum: float32 [16, 448, 1, 4608], P('rep', 'fsdp'), may hold values from -6 to 6
- weight: bfloat16 [448, 1, 4608], P('fsdp'), may hold values from -0.25 to 0.25
- next_acts: bfloat16 [1, 98304, 448], P(None, ('rep', 'fsdp')), may hold values from -6 to 6
Outputs:
- next_out: bfloat16 [1, 98304, 4608], P(None, ('rep', 'fsdp'))
- new_momentum: float32 [16, 448, 1, 4608], P('rep', 'fsdp')
All inputs are finite; a program needn't handle non-finite values.
Results may differ from a plain program's by a relative error of at most 0.02.
Values may be sent and summed in bfloat16 or wider, within the bound.
A program may use at most 128 MiB of HBM per device.

v0:
```python
import math

import jax
import jax.numpy as jnp
from jax import lax
from jax.sharding import PartitionSpec as P

SPAN = 256
KEEP = 32


def cosine_table(length, kept_count):
    frequency = jnp.arange(kept_count, dtype=jnp.float32)[:, None]
    sample = jnp.arange(length, dtype=jnp.float32)[None, :]
    cosines = jnp.cos(jnp.pi * (2.0 * sample + 1.0) * frequency / (2.0 * length)) * jnp.sqrt(
        2.0 / length
    )
    return jnp.where(frequency == 0.0, cosines * jnp.sqrt(0.5), cosines)


def encode(values, cosine_rows):
    shaped = values.reshape(
        values.shape[:-1] + (values.shape[-1] // cosine_rows.shape[1], cosine_rows.shape[1])
    )
    return jnp.einsum("...c,kc->...k", shaped, cosine_rows, precision=lax.Precision.HIGHEST)


def decode(coeffs, cosine_rows):
    shaped = jnp.einsum("...k,kc->...c", coeffs, cosine_rows, precision=lax.Precision.HIGHEST)
    return shaped.reshape(shaped.shape[:-2] + (shaped.shape[-2] * shaped.shape[-1],))


def local(hid_acts, out_cot, momentum, weight, next_acts):
    group_tokens = hid_acts.shape[1] * lax.axis_size("fsdp")
    norm_factor = 1.0 / math.sqrt(group_tokens)
    columns = hid_acts
    grad = lax.psum_scatter(
        (
            jnp.einsum("ltr,ltd->rld", columns, out_cot, preferred_element_type=jnp.float32)
            * norm_factor
        ).astype(jnp.bfloat16),
        "fsdp",
        scatter_dimension=0,
        tiled=True,
    ).astype(jnp.float32)
    blended = 0.9 * momentum[0] + grad
    cosine_rows = cosine_table(SPAN, KEEP)
    coeffs = encode(blended, cosine_rows)
    new_momentum = (blended - decode(coeffs, cosine_rows))[None]
    mean_coeffs = lax.psum(coeffs, "rep") / lax.axis_size("rep")
    new_weight = (weight.astype(jnp.float32) - 0.5 * decode(mean_coeffs, cosine_rows)).astype(
        jnp.bfloat16
    )
    columns = next_acts
    produced = jnp.einsum(
        "ltr,rld->ltd",
        columns,
        lax.all_gather(new_weight, "fsdp", axis=0, tiled=True),
        preferred_element_type=jnp.float32,
    )
    return (produced.astype(jnp.bfloat16), new_momentum)


def solution(mesh):
    return jax.shard_map(
        local,
        mesh=mesh,
        in_specs=(
            P(None, ("rep", "fsdp"), None),
            P(None, ("rep", "fsdp"), None),
            P("rep", "fsdp", None, None),
            P("fsdp", None, None),
            P(None, ("rep", "fsdp"), None),
        ),
        out_specs=(P(None, ("rep", "fsdp"), None), P("rep", "fsdp", None, None)),
        check_vma=False,
    )
```

profile of v0, /device:TPU:1, one launch (start us, length us, event | category | flops | bytes accessed | tf_op | source)
XLA Modules:
  0.0 305.0 jit_solution(6191776400048552501)
XLA Ops:
  7.2 0.0 copy-start
  7.2 0.0 all-gather.2.cloned.1.call-start
  7.2 1.4 copy-done
  8.6 4.1 %fusion.1 = bf16[448,1,4608]{2,0,1:T(8,128)(2,1)} fusion(bf16[1,192,4608]{2,1,0:T(8,128)(2,1)S(1)} %copy-done, bf16[1,192,448]{2,1,0:T(8,128)(2,1)} %param.5), kind=kOutput, calls=%fused_computation.1 | convolution fusion | flops 796852224 | bytes 6070272 | tf_op jit(solution)/shard_map/ltr,ltd->rld/dot_general | solution.py:39
  12.8 84.2 %fusion = bf16[16,4608]{1,0:T(8,128)(2,1)S(1)} fusion(bf16[448,1,4608]{2,0,1:T(8,128)(2,1)} %fusion.1), kind=kCustom, calls=%all-reduce-scatter | all-reduce-scatter fusion | flops 2359297 | bytes 4278272
  97.0 1.9 collective-permute-start
  98.9 1.3 collective-permute-start.1
  100.2 1.3 collective-permute-start.2
  101.6 1.3 collective-permute-start.3
  102.9 1.3 dynamic-slice.4
  104.8 0.3 collective-permute-done.3
  105.2 0.0 collective-permute-done
  105.2 0.0 collective-permute-done.1
  105.2 0.0 collective-permute-done.2
  105.2 1.5 concatenate
  106.7 0.0 copy-done.1
  106.7 0.1 bitcast_add_fusion
  106.8 0.0 copy-start.2
  106.8 0.1 reshape.85
  106.9 0.5 fusion.14
  107.4 56.3 %psum.7 = f32[14,1,18,32]{3,2,0,1:T(8,128)S(1)} all-reduce(f32[14,1,18,32]{3,2,0,1:T(8,128)S(1)} %bitcast.47), channel_id=1, replica_groups=mesh['rep'=16,'fsdp'=32] {'rep'}, use_global_device_ids=true, to_apply=%region_1.2 | all-reduce | flops 8064 | bytes 64512 | tf_op jit(solution)/shard_map/psum | solution.py:50
  163.7 0.5 convolution_multiply_fusion
  164.2 0.1 mul.135
  164.3 0.9 subtract_convert_fusion
  165.2 0.9 copy.15
  166.1 0.0 all-gather.2.cloned.1.call-update
  166.2 0.5 fusion.11
  166.7 0.1 reshape.89
  166.8 1.0 copy.16
  167.8 124.8 %all-gather.2.cloned.1.call-done = bf16[448,1,4608]{2,1,0:T(2,128)(2,1)} async-done(((bf16[14,1,4608]{2,1,0:T(2,128)(2,1)}), bf16[448,1,4608]{2,1,0:T(2,128)(2,1)}) %all-gather.2.cloned.1.call-update) | async-done | bytes 4128784 | tf_op jit(solution)/shard_map/all_gather | solution.py:58
  292.6 0.0 copy-done.2
  292.6 5.6 %fusion.2 = bf16[1,192,4608]{2,1,0:T(8,128)(2,1)} fusion(bf16[448,1,4608]{2,1,0:T(2,128)(2,1)} %all-gather.2.cloned.1.call-done, bf16[1,192,448]{2,1,0:T(8,128)(2,1)S(1)} %copy-done.2), kind=kOutput, calls=%fused_computation.3 | convolution fusion | flops 793608192 | bytes 6070272 | tf_op jit(solution)/shard_map/ltr,rld->ltd/dot_general | solution.py:55
  (5 shorter events, 0.1 us)
Async XLA Ops:
  7.2 1.5 copy-start
  7.2 285.4 %all-gather.2.cloned.1.call-start = ((), (), s32[]{:S(2)}) async-start(), calls=%async_computation | async-start | bytes 8515584 | tf_op jit(solution)/shard_map/all_gather | solution.py:58
  12.8 93.9 %copy-start.1 = (f32[1,14,1,4608]{3,2,1,0:T(1,128)S(1)}, f32[1,14,1,4608]{3,2,1,0:T(1,128)}, u32[]{:S(2)}) copy-start(f32[1,14,1,4608]{3,2,1,0:T(1,128)} %param.7) | copy-start | bytes 774148
  97.0 8.2 %collective-permute-start = (bf16[16,4608]{1,0:T(8,128)(2,1)S(1)}, bf16[16,4608]{1,0:T(8,128)(2,1)S(1)}, u32[]{:S(2)}, u32[]{:S(2)}) collective-permute-start(bf16[16,4608]{1,0:T(8,128)(2,1)S(1)} %fusion), channel_id=1, source_target_pairs={{0,1},{1,2},{2,3},{3,4},{4,5},{5,6},{6,7},{7,8},{8,9},{9,10},{10,1... | collective-permute-start | bytes 442376
  98.9 6.3 %collective-permute-start.1 = (bf16[16,4608]{1,0:T(8,128)(2,1)S(1)}, bf16[16,4608]{1,0:T(8,128)(2,1)S(1)}, u32[]{:S(2)}, u32[]{:S(2)}) collective-permute-start(bf16[16,4608]{1,0:T(8,128)(2,1)S(1)} %fusion), channel_id=1, source_target_pairs={{0,2},{1,3},{2,4},{3,5},{4,6},{5,7},{6,8},{7,9},{8,10},{9,11},{10,... | collective-permute-start | bytes 442376
  100.2 5.0 %collective-permute-start.2 = (bf16[16,4608]{1,0:T(8,128)(2,1)S(1)}, bf16[16,4608]{1,0:T(8,128)(2,1)S(1)}, u32[]{:S(2)}, u32[]{:S(2)}) collective-permute-start(bf16[16,4608]{1,0:T(8,128)(2,1)S(1)} %fusion), channel_id=1, source_target_pairs={{0,3},{1,4},{2,5},{3,6},{4,7},{5,8},{6,9},{7,10},{8,11},{9,12},{10... | collective-permute-start | bytes 442376
  101.6 3.6 %collective-permute-start.3 = (bf16[14,4608]{1,0:T(8,128)(2,1)S(1)}, bf16[14,4608]{1,0:T(8,128)(2,1)S(1)}, u32[]{:S(2)}, u32[]{:S(2)}) collective-permute-start(bf16[14,4608]{1,0:T(8,128)(2,1)S(1)} %slice), channel_id=1, source_target_pairs={{0,4},{1,5},{2,6},{3,7},{4,8},{5,9},{6,10},{7,11},{8,12},{9,13},{1... | collective-permute-start | bytes 387080
  106.8 185.8 %copy-start.2 = (bf16[1,192,448]{2,1,0:T(8,128)(2,1)S(1)}, bf16[1,192,448]{2,1,0:T(8,128)(2,1)}, u32[]{:S(2)}) copy-start(bf16[1,192,448]{2,1,0:T(8,128)(2,1)} %param.9) | copy-start | bytes 516100
Sparse Core Ops, SparseCore 0:
  166.3 126.2 all-gather.1
where the time goes:
time: 305 us
  blocking collectives  140 us (46%)
  waiting for transfers between devices  125 us (41%)
  between operations  14.8 us (5%)
  matrix products  11.4 us (4%)
  local copies, waits for them, and re-layouts  6.31 us (2%)
  starting transfers between devices  5.88 us (2%)
    all_gather x1, waiting for transfers between devices, local(): lax.all_gather(new_weight, 'fsdp', axis=0, tiled=True)  125 us
    unnamed x1, blocking collectives  84.2 us
    psum x1, blocking collectives, local(): mean_coeffs = lax.psum(coeffs, 'rep') / lax.axis_size('rep')  56.3 us
  transfers between devices with their start and end apart: 5, of which 2 were waited for; matrix products, arithmetic and copies ran while one was open for 1% of the time, Pallas kernels for 0%

commit v1 on v0

v1 whole, which is shorter than its diff:
```python
import math

import jax
import jax.numpy as jnp
import numpy as np
from jax import lax
from jax.experimental import pallas as pl
from jax.experimental.pallas import tpu as pltpu
from jax.sharding import PartitionSpec as P

SPAN = 256
KEEP = 32
HIGH = SPAN - KEEP
TOK = 192
ROWS = 448
D = 4608
BLOCKS = D // SPAN
OWN = 14
HALF = 224
NY, NZ, NX = 8, 8, 4
SLICE = D // 4
LOW_AT = 4096
CT = LOW_AT + 640
NORM = 1.0 / math.sqrt(TOK * 32)
F32, BF16 = jnp.float32, jnp.bfloat16
HI = lax.Precision.HIGHEST


def tables():
    k = np.arange(SPAN, dtype=np.float64)[:, None]
    n = np.arange(SPAN, dtype=np.float64)[None, :]
    dct = np.cos(np.pi * (2.0 * n + 1.0) * k / (2.0 * SPAN)) * np.sqrt(2.0 / SPAN)
    dct[0] *= np.sqrt(0.5)
    low, high = dct[:KEEP], dct[KEEP:]
    forward = np.concatenate([high, low], axis=0).T
    back = np.concatenate([high, np.zeros((KEEP, SPAN))], axis=0)
    low_t = np.tile(low.T, (1, 4))
    diag = np.zeros((128, 1024))
    for i in range(4):
        diag[32 * i : 32 * i + 32, 256 * i : 256 * i + 256] = low
    diag = np.concatenate([diag, diag], axis=0)
    return (
        jnp.asarray(forward, BF16),
        jnp.asarray(back, BF16),
        jnp.asarray(low_t, F32),
        jnp.asarray(low, F32),
        jnp.asarray(diag, BF16),
    )


def dot(a, b, contract=((1,), (0,)), precision=None):
    return lax.dot_general(
        a, b, (contract, ((), ())), precision=precision, preferred_element_type=F32
    )


def iota(shape, dim):
    return lax.broadcasted_iota(jnp.int32, shape, dim)


def cdiv14(w):
    return (w >= 14).astype(jnp.int32)


FOUND = ((0,), (-1, 1), (-2, 2), (-3, 3), (-4,))
UP = (0, -1, -2, -3)


def slot_of(o):
    return o + 4


def kernel(
    hid_h, cot_h, mom_h, w_h, act_h, fwd_h, back_h, lowt_h, low_h, diag_h,
    out_ref, nm_ref,
    cot, hid, acts, mom, wraw, fwd, back, lowt, low, diag,
    ct, lowf, lhs, gram, parts, ring, xs, xr, keep, m2, nm2, high8,
    wsh, wx, wbuf, cbuf, cxr, cx, czr, cz, cyr, mbuf, call, actw, actc, acc,
    lsem, hid_s, ct_s, ring_s, x2_s, w0_s, wy_s, wza_s, wzb_s, wzf_s, wxx_s, wsib_s,
    c1_s, c2_s, c3_s, c4_s, c5_s, c6_s,
):
    rep, f = lax.axis_index("rep"), lax.axis_index("fsdp")
    xlo, z = rep // NZ, rep % NZ
    y, xhi, c = f // 4, (f // 2) % 2, f % 2
    x = xhi * 2 + xlo

    def dev(dx=0, dy=0, dz=0, dc=0):
        xx, yy, zz, cc = (x + dx + NX) % NX, (y + dy + NY) % NY, (z + dz + NZ) % NZ, (c + dc) % 2
        return ((xx % 2) * NZ + zz, (yy * 2 + xx // 2) * 2 + cc)

    pending = []

    def send(src, dst, sems, index, to):
        copy = pltpu.make_async_remote_copy(
            src_ref=src, dst_ref=dst, send_sem=sems.at[(0,) + index], recv_sem=sems.at[(1,) + index],
            device_id=to, device_id_type=pl.DeviceIdType.MESH,
        )
        copy.start()
        pending.append(copy)

    def wait(dst, sems, index):
        pltpu.make_async_remote_copy(
            src_ref=dst, dst_ref=dst, send_sem=sems.at[(0,) + index], recv_sem=sems.at[(1,) + index],
            device_id=dev(dc=1), device_id_type=pl.DeviceIdType.MESH,
        ).wait_recv()

    loads = {}
    for i, (name, src, dst) in enumerate((
        ("w", w_h, wraw), ("hid", hid_h.at[0], hid.at[pl.ds(0, TOK)]), ("fwd", fwd_h, fwd),
        ("cot", cot_h.at[0], cot), ("mom", mom_h, mom), ("lowt", lowt_h, lowt), ("low", low_h, low),
        ("acts", act_h.at[0], acts), ("back", back_h, back), ("diag", diag_h, diag),
    )):
        loads[name] = pltpu.make_async_copy(src, dst, lsem.at[i])
        loads[name].start()

    barrier = pltpu.get_barrier_semaphore()
    friends = [dev(dc=1)]
    friends += [dev(dy=i) for i in range(1, NY)]
    friends += [dev(dz=i) for i in range(1, NZ)]
    friends += [dev(dx=i) for i in range(1, NX)]
    for friend in friends:
        pl.semaphore_signal(barrier, inc=1, device_id=friend, device_id_type=pl.DeviceIdType.MESH)

    loads["w"].wait()
    wsh[...] = jnp.concatenate([wraw[...], jnp.zeros((2, D), BF16)], axis=0)
    m2[...] = jnp.zeros_like(m2)
    loads["mom"].wait()
    for b in range(BLOCKS):
        for h in range(2):
            m2[pl.ds(16 * b, OWN), pl.ds(128 * h, 128)] = mom[pl.ds(2 * b + h, OWN, stride=36), :]

    pl.semaphore_wait(barrier, len(friends))

    sig = z % 4
    kap = xlo

    def cols(s):
        return pl.ds(pl.multiple_of(((s + 4) % 4) * SLICE, 128), SLICE)

    def wslice(o, s, k=None):
        return wbuf.at[c, kap if k is None else k, (y + o + NY) % NY, :, cols(s)]

    def wfull(o, k, core=None):
        return wbuf.at[c if core is None else core, k, (y + o + NY) % NY]

    cross = lax.rem(x + 3 * (1 - xlo) + xlo, NX)
    cross_dev = ((cross % 2) * NZ + z, (y * 2 + cross // 2) * 2 + c)
    loads["hid"].wait()
    send(hid.at[pl.ds(0, TOK)], hid.at[pl.ds(TOK, TOK)], hid_s, (0,), dev(dc=1))
    send(wsh.at[:, cols(sig)], wx, w0_s, (0,), cross_dev)

    loads["fwd"].wait()
    loads["cot"].wait()
    lane = iota((TOK, 128), 1)
    table = fwd[...]
    seen = set()

    def transform(b):
        full = dot(cot[:, pl.ds(SPAN * b, SPAN)], table)
        first, second = full[:, :128], full[:, 128:]
        u, place = b // 4, 32 * (b % 4)
        turned = pltpu.roll(second, (place - 96) % 128, 1) if place != 96 else second
        mine = (lane >= place) & (lane < place + 32)
        at = pl.ds(128 * u, 128)
        lowf[:, at] = jnp.where(mine, turned, lowf[:, at] if u in seen else 0.0)
        seen.add(u)
        return first, second

    for h in range(2):
        first, second = transform(9 * h + 8)
        high8[h, :, pl.ds(0, 128)] = first
        high8[h, :, pl.ds(128, 128)] = second
    for s in range(4):
        for q in range(4):
            h, j = q // 2, 4 * (q % 2) + s
            first, second = transform(9 * h + j)
            if j < 7:
                extra = high8[h, :, pl.ds(128 * (j // 4), 128)]
                shift = (96 - 32 * (j % 4)) % 128
                extra = pltpu.roll(extra, shift, 1) if shift else extra
            else:
                extra = jnp.zeros_like(second)
            at = 1024 * s + 256 * q
            ct[pl.ds(0, TOK), pl.ds(at, 128)] = first.astype(BF16)
            ct[pl.ds(0, TOK), pl.ds(at + 128, 128)] = jnp.where(lane < 96, second, extra).astype(BF16)
        part = pl.ds(1024 * s, 1024)
        send(ct.at[pl.ds(0, TOK), part], ct.at[pl.ds(TOK, TOK), part], ct_s, (s,), dev(dc=1))
    ct[pl.ds(0, TOK), pl.ds(LOW_AT, 640)] = lowf[...].astype(BF16)
    part = pl.ds(LOW_AT, 640)
    send(ct.at[pl.ds(0, TOK), part], ct.at[pl.ds(TOK, TOK), part], ct_s, (4,), dev(dc=1))

    wait(wx, w0_s, (0,))
    own = wsh[:, cols(sig)]
    wslice(0, sig)[...] = jnp.where(jnp.broadcast_to(kap == xhi, own.shape), own, wx[...])

    def wy_send(k):
        send(wslice(1 - k, sig), wslice(1 - k, sig), wy_s, (0, k - 1), dev(dy=1))
        if k < 4:
            send(wslice(k - 1, sig), wslice(k - 1, sig), wy_s, (1, k - 1), dev(dy=-1))

    def wy_wait(k):
        wait(wslice(-k, sig), wy_s, (0, k - 1))
        if k < 4:
            wait(wslice(k, sig), wy_s, (1, k - 1))

    def wz_send(k):
        for o in FOUND[k]:
            send(wslice(o, sig), wslice(o, sig), wza_s, (slot_of(o),), dev(dz=1))
            send(wslice(o, sig), wslice(o, sig), wzb_s, (slot_of(o),), dev(dz=-1))

    def wz_pass(k):
        for o in FOUND[k]:
            wait(wslice(o, sig - 1), wza_s, (slot_of(o),))
            wait(wslice(o, sig + 1), wzb_s, (slot_of(o),))
            if o in UP:
                send(wslice(o, sig - 1), wslice(o, sig - 1), wzf_s, (slot_of(o),), dev(dz=1))
            else:
                send(wslice(o, sig + 1), wslice(o, sig + 1), wzf_s, (slot_of(o),), dev(dz=-1))

    def wx_send(k):
        for o in FOUND[k]:
            wait(wslice(o, sig + 2), wzf_s, (slot_of(o),))
            send(wfull(o, kap), wfull(o, kap), wxx_s, (slot_of(o),), dev(dx=1 if o in UP else -1))
            send(wfull(o, kap), wfull(o, kap), wsib_s, (0, slot_of(o)), dev(dc=1))

    def wx_wait(k):
        for o in FOUND[k]:
            wait(wfull(o, 1 - kap), wxx_s, (slot_of(o),))
            send(wfull(o, 1 - kap), wfull(o, 1 - kap), wsib_s, (1, slot_of(o)), dev(dc=1))

    def wsib_wait(k):
        for o in FOUND[k]:
            wait(wfull(o, kap, 1 - c), wsib_s, (0, slot_of(o)))
            wait(wfull(o, 1 - kap, 1 - c), wsib_s, (1, slot_of(o)))

    def w_step(i):
        if 1 <= i <= 4:
            wy_wait(i)
            if i < 4:
                wy_send(i + 1)
            wz_send(i)
        if 0 <= i - 1 <= 4:
            wz_pass(i - 1)
        if 0 <= i - 2 <= 4:
            wx_send(i - 2)
        if 0 <= i - 3 <= 4:
            wx_wait(i - 3)

    wy_send(1)
    wz_send(0)

    wait(hid.at[pl.ds(TOK, TOK)], hid_s, (0,))
    both = hid[...]
    for at, rows, width, lead in ((0, 256, 32, 0), (256, 256, 32, 4), (512, 224, 28, 0)):
        for g in range(NY):
            row, col = iota((width, ROWS), 0), iota((width, ROWS), 1)
            w = row - lead
            good = (w >= 0) & (w < 28)
            target = 56 * g + 14 * c + w + 14 * cdiv14(w)
            gram[pl.ds(0, width), pl.ds(0, ROWS)] = jnp.where(good & (col == target), 1.0, 0.0)
            lhs[pl.ds(at + width * g, width)] = dot(
                gram[pl.ds(0, width), pl.ds(0, ROWS)].astype(BF16), both, ((1,), (1,))
            )
    left = [lhs[pl.ds(256 * i, 256)].astype(BF16) for i in range(2)]

    def ring_send(s, k):
        d = 1 if s % 2 == 0 else -1
        src = parts.at[s, (y - d + NY) % NY] if k == 0 else ring.at[s, k - 1]
        send(src, ring.at[s, k], ring_s, (s, k), dev(dy=d))

    def ring_step(s, k):
        d = 1 if s % 2 == 0 else -1
        wait(ring.at[s, k], ring_s, (s, k))
        owner = (y - d * (2 + k) + 2 * NY) % NY
        total = ring[s, k].astype(F32) + parts[s, owner].astype(F32)
        ring[s, k] = total.astype(BF16)
        if k < 6:
            ring_send(s, k + 1)

    for s in range(4):
        wait(ct.at[pl.ds(TOK, TOK), pl.ds(1024 * s, 1024)], ct_s, (s,))
        for q in range(4):
            gram[pl.ds(256 * q, 256), pl.ds(0, 256)] = (
                dot(left[q % 2], ct[:, pl.ds(1024 * s + 256 * q, 256)]) * NORM
            )
        for g in range(NY):
            pieces = []
            for pair in range(2):
                a = gram[pl.ds(512 * pair + 32 * g, 32), pl.ds(0, 256)]
                b = gram[pl.ds(512 * pair + 256 + 32 * g, 32), pl.ds(0, 256)]
                pieces += [a[:24], a[24:] + b[:8], b[8:]]
            parts[s, g] = jnp.concatenate(pieces, axis=0).astype(BF16)
        ring_send(s, 0)

    loads["lowt"].wait()
    loads["low"].wait()
    mine = m2[...]
    kept = dot(mine, lowt[...], precision=HI)
    nm2[...] = 0.9 * (mine - dot(kept[:, :KEEP], low[...], precision=HI))
    lane16 = iota((16, 128), 1)
    tiles = []
    for u in range(5):
        tile = jnp.zeros((16, 128), F32)
        for i in range(4):
            b = 4 * u + i
            if b < BLOCKS:
                good = (lane16 >= 32 * i) & (lane16 < 32 * i + 32)
                tile = jnp.where(good, 0.9 * kept[16 * b : 16 * b + 16], tile)
        tiles.append(tile)
    spread = jnp.concatenate(tiles, axis=1)
    row, col = iota((HALF, 16), 0), iota((HALF, 16), 1)
    place = jnp.where((row == OWN * (2 * y + xhi) + col) & (col < OWN), 1.0, 0.0)
    wait(ct.at[pl.ds(TOK, TOK), pl.ds(LOW_AT, 640)], ct_s, (4,))
    local = dot(lhs[pl.ds(512, HALF)].astype(BF16), ct[:, pl.ds(LOW_AT, 640)]) * NORM
    local = local + dot(place, spread, precision=HI)
    for rt in range(14):
        for u in range(4):
            cbuf[4 * rt + u] = local[16 * rt : 16 * rt + 16, 128 * u : 128 * u + 128].astype(BF16)
    for i in range(7):
        a = local[32 * i : 32 * i + 16, 512:640]
        b = local[32 * i + 16 : 32 * i + 32, 512:640]
        cbuf[56 + i] = jnp.where(lane16 < 64, a, pltpu.roll(b, 64, 1)).astype(BF16)
    cbuf[63] = jnp.zeros((16, 128), BF16)

    def c1_send():
        for i in range(1, NX):
            to = (x + i) % NX
            send(cbuf.at[pl.ds(16 * to, 16)], cxr.at[i - 1], c1_s, (i - 1,), dev(dx=i))

    def c2_send():
        total = cbuf[pl.ds(16 * x, 16)].astype(F32)
        for i in range(1, NX):
            wait(cxr.at[i - 1], c1_s, (i - 1,))
            total = total + cxr[i - 1].astype(F32)
        cx[...] = total.astype(BF16)
        for i in range(1, NZ):
            send(cx.at[pl.ds(2 * ((z + i) % NZ), 2)], czr.at[i - 1], c2_s, (i - 1,), dev(dz=i))

    def c3_send():
        total = cx[pl.ds(2 * z, 2)].astype(F32)
        for i in range(1, NZ):
            wait(czr.at[i - 1], c2_s, (i - 1,))
            total = total + czr[i - 1].astype(F32)
        cz[...] = total.astype(BF16)
        for i in range(1, NY):
            send(cz, cyr.at[i - 1], c3_s, (i - 1,), dev(dy=i))

    def piece(zz):
        return mbuf.at[c, pl.ds(16 * x + 2 * ((zz + NZ) % NZ), 2)]

    def c4_send():
        total = cz[...].astype(F32)
        for i in range(1, NY):
            wait(cyr.at[i - 1], c3_s, (i - 1,))
            total = total + cyr[i - 1].astype(F32)
        piece(z)[...] = (total * (1.0 / 16.0)).astype(BF16)
        for i in range(1, NZ):
            send(piece(z), piece(z), c4_s, (i - 1,), dev(dz=i))

    def strip(xx, core):
        return mbuf.at[core, pl.ds(16 * ((xx + NX) % NX), 16)]

    def c5_send():
        for i in range(1, NZ):
            wait(piece(z - i), c4_s, (i - 1,))
        for i in range(1, NX):
            send(strip(x, c), strip(x, c), c5_s, (i - 1,), dev(dx=i))
        send(strip(x, c), strip(x, c), c6_s, (0,), dev(dc=1))

    def c6_send():
        for i in range(1, NX):
            wait(strip(x - i, c), c5_s, (i - 1,))
            send(strip(x - i, c), strip(x - i, c), c6_s, (i,), dev(dc=1))

    def c_done():
        for i in range(NX):
            wait(strip(x - i, 1 - c), c6_s, (i,))

    c1_send()

    loads["acts"].wait()
    a = acts[...]
    row, col = iota((ROWS, HALF), 0), iota((ROWS, HALF), 1)
    for core in range(2):
        pick = jnp.zeros((ROWS, HALF), F32)
        for g in range(NY):
            w = col - 28 * g
            good = (w >= 0) & (w < 28)
            target = 56 * g + 14 * core + w + 14 * cdiv14(w)
            pick = jnp.where(good & (row == target), 1.0, pick)
        actc[core] = dot(a, pick.astype(BF16)).astype(BF16)
        row2, col2 = iota((ROWS, 256), 0), iota((ROWS, 256), 1)
        j, t = col2 % 16, col2 // 16
        target = 56 * (t % 8) + 28 * (t // 8) + 14 * core + j
        pick = jnp.where((j < OWN) & (row2 == target), 1.0, 0.0)
        actw[:, pl.ds(256 * core, 256)] = dot(a, pick.astype(BF16)).astype(BF16)

    def ring_all(k):
        for s in range(4):
            ring_step(s, k)

    ring_all(0)
    w_step(1)
    ring_all(1)
    c2_send()
    w_step(2)
    ring_all(2)
    c3_send()
    w_step(3)
    ring_all(3)
    c4_send()
    w_step(4)
    ring_all(4)
    c5_send()
    w_step(5)
    ring_all(5)
    w_step(6)
    c6_send()

    row, col = iota((64, 112), 0), iota((64, 112), 1)
    j, q16 = row % 16, row // 16

    def pick_rows(hi):
        return jnp.where((j < OWN) & (col == 28 * q16 + 14 * hi + j), 1.0, 0.0).astype(BF16)

    for s in range(4):
        ring_step(s, 6)
        chunk = ring[s, 6]
        xs[s] = dot(pick_rows(1 - xhi), chunk).astype(BF16)
        send(xs.at[s], xr.at[s], x2_s, (s,), dev(dx=2))
        keep[s] = dot(pick_rows(xhi), chunk)

    w_step(7)
    for k in range(5):
        wsib_wait(k)
    for core in range(2):
        for t in range(4):
            at = pl.ds(SLICE * t, SLICE)
            term = dot(actw[:, pl.ds(256 * core, 256)], wbuf[core, :, :, :, at].reshape(256, SLICE))
            acc[:, at] = term if core == 0 else acc[:, at] + term

    c_done()
    loads["diag"].wait()
    for core in range(2):
        for rt in range(14):
            for u in range(4):
                call[pl.ds(HALF * core + 16 * rt, 16), pl.ds(128 * u, 128)] = mbuf[core, 4 * rt + u]
        for i in range(7):
            tile = mbuf[core, 56 + i].astype(F32)
            at = HALF * core + 32 * i
            call[pl.ds(at, 16), pl.ds(512, 128)] = jnp.where(lane16 < 64, tile, 0.0).astype(BF16)
            call[pl.ds(at + 16, 16), pl.ds(512, 128)] = jnp.where(
                lane16 < 64, pltpu.roll(tile, 64, 1), 0.0
            ).astype(BF16)
    inner = dot(actc[0], call[pl.ds(0, HALF)]) + dot(actc[1], call[pl.ds(HALF, HALF)])
    inner = inner * 0.5
    top = inner.astype(BF16)
    rest = (inner - top.astype(F32)).astype(BF16)
    for u in range(5):
        width = 1024 if u < 4 else 512
        at = pl.ds(1024 * u, width)
        pair = jnp.concatenate([top[:, 128 * u : 128 * u + 128], rest[:, 128 * u : 128 * u + 128]], axis=1)
        out_ref[:, at] = (acc[:, at] - dot(pair, diag[:, pl.ds(0, width)])).astype(BF16)

    loads["back"].wait()
    inverse = back[...]
    eights = [[jnp.zeros((16, 128), F32) for _ in range(2)] for _ in range(2)]

    def to_space(values):
        big = values.astype(BF16)
        return dot(big, inverse) + dot((values - big.astype(F32)).astype(BF16), inverse)

    for s in range(4):
        wait(xr.at[s], x2_s, (s,))
        total = keep[s] + xr[s].astype(F32)
        space = to_space(total)
        for q in range(4):
            h, j = q // 2, 4 * (q % 2) + s
            at = pl.ds(16 * (9 * h + j), 16)
            nm2[at] = nm2[at] + space[16 * q : 16 * q + 16]
            if j < 7:
                tail = total[16 * q : 16 * q + 16, 128:]
                place = 32 * (j % 4)
                tail = pltpu.roll(tail, (place - 96) % 128, 1) if place != 96 else tail
                good = (lane16 >= place) & (lane16 < place + 32)
                eights[h][j // 4] = jnp.where(good, tail, eights[h][j // 4])
    for h in range(2):
        at = pl.ds(16 * (9 * h + 8), 16)
        nm2[at] = nm2[at] + to_space(jnp.concatenate(eights[h], axis=1))
    for b in range(BLOCKS):
        for h in range(2):
            nm_ref[pl.ds(2 * b + h, OWN, stride=36), :] = nm2[pl.ds(16 * b, OWN), pl.ds(128 * h, 128)]

    for copy in pending:
        copy.wait_send()


def local(hid_acts, out_cot, momentum, weight, next_acts):
    any_space = pl.BlockSpec(memory_space=pl.ANY)
    vmem = pl.BlockSpec(memory_space=pltpu.VMEM)
    dma = pltpu.SemaphoreType.DMA
    scratch = [
        pltpu.VMEM((TOK, D), BF16),
        pltpu.VMEM((2 * TOK, ROWS), BF16),
        pltpu.VMEM((TOK, ROWS), BF16),
        pltpu.VMEM((504, 128), F32),
        pltpu.VMEM((OWN, D), BF16),
        pltpu.VMEM((SPAN, SPAN), BF16),
        pltpu.VMEM((SPAN, SPAN), BF16),
        pltpu.VMEM((SPAN, 128), F32),
        pltpu.VMEM((KEEP, SPAN), F32),
        pltpu.VMEM((SPAN, 1024), BF16),
        pltpu.VMEM((2 * TOK, CT), BF16),
        pltpu.VMEM((TOK, 640), F32),
        pltpu.VMEM((736, 2 * TOK), F32),
        pltpu.VMEM((1024, 512), F32),
        pltpu.VMEM((4, NY, 112, 256), BF16),
        pltpu.VMEM((4, 7, 112, 256), BF16),
        pltpu.VMEM((4, 64, 256), BF16),
        pltpu.VMEM((4, 64, 256), BF16),
        pltpu.VMEM((4, 64, 256), F32),
        pltpu.VMEM((16 * BLOCKS, SPAN), F32),
        pltpu.VMEM((16 * BLOCKS, SPAN), F32),
        pltpu.VMEM((2, TOK, SPAN), F32),
        pltpu.VMEM((16, D), BF16),
        pltpu.VMEM((16, SLICE), BF16),
        pltpu.VMEM((2, 2, NY, 16, D), BF16),
        pltpu.VMEM((64, 16, 128), BF16),
        pltpu.VMEM((3, 16, 16, 128), BF16),
        pltpu.VMEM((16, 16, 128), BF16),
        pltpu.VMEM((7, 2, 16, 128), BF16),
        pltpu.VMEM((2, 16, 128), BF16),
        pltpu.VMEM((7, 2, 16, 128), BF16),
        pltpu.VMEM((2, 64, 16, 128), BF16),
        pltpu.VMEM((ROWS, 640), BF16),
        pltpu.VMEM((TOK, 512), BF16),
        pltpu.VMEM((2, TOK, HALF), BF16),
        pltpu.VMEM((TOK, D), F32),
        dma((10,)),
        dma((2, 1)),
        dma((2, 5)),
        dma((2, 4, 7)),
        dma((2, 4)),
        dma((2, 1)),
        dma((2, 2, 4)),
        dma((2, 8)),
        dma((2, 8)),
        dma((2, 8)),
        dma((2, 8)),
        dma((2, 2, 8)),
        dma((2, 3)),
        dma((2, 7)),
        dma((2, 7)),
        dma((2, 7)),
        dma((2, 3)),
        dma((2, 4)),
    ]
    out, nm = pl.pallas_call(
        kernel,
        out_shape=(
            jax.ShapeDtypeStruct((TOK, D), BF16),
            jax.ShapeDtypeStruct((504, 128), F32),
        ),
        in_specs=[any_space] * 10,
        out_specs=(vmem, vmem),
        scratch_shapes=scratch,
        compiler_params=pltpu.CompilerParams(
            collective_id=0, has_side_effects=True, vmem_limit_bytes=56 * 2**20
        ),
        name="step",
    )(
        hid_acts,
        out_cot,
        momentum.reshape(504, 128),
        weight.reshape(OWN, D),
        next_acts,
        *tables(),
    )
    return out[None], nm.reshape(1, OWN, 1, D)


def solution(mesh):
    return jax.shard_map(
        local,
        mesh=mesh,
        in_specs=(
            P(None, ("rep", "fsdp"), None),
            P(None, ("rep", "fsdp"), None),
            P("rep", "fsdp", None, None),
            P("fsdp", None, None),
            P(None, ("rep", "fsdp"), None),
        ),
        out_specs=(P(None, ("rep", "fsdp"), None), P("rep", "fsdp", None, None)),
        check_vma=False,
    )
```

time: 305 us -> 67.6 us (0.22)
  blocking collectives: 140 us -> 0 us
  waiting for transfers between devices: 125 us -> 0 us
  Pallas kernels: 0 us -> 63.3 us
  between operations: 14.8 us -> 0.65 us
  matrix products: 11.4 us -> 0 us
  starting transfers between devices: 5.88 us -> 0 us
    all_gather x1 -> x0, waiting for transfers between devices: 125 us -> none  [local(): lax.all_gather(new_weight, 'fsdp', axis=0, tiled=True)]
    unnamed x1 -> x0, blocking collectives: 84.2 us -> none
    pallas_call x0 -> x1, Pallas kernels: none -> 63.3 us  [local(): pl.pallas_call(kernel, out_shape=(jax.ShapeDtypeStruct((TOK, D), BF16), j...]
    psum x1 -> x0, blocking collectives: 56.3 us -> none  [local(): mean_coeffs = lax.psum(coeffs, 'rep') / lax.axis_size('rep')]
    dot_general x5 -> x0, matrix products: 11.4 us -> none  [the longest x1 5.64 us: local(): jnp.einsum('ltr,rld->ltd', columns, lax.all_gather(new_weight, 'fsdp', ax...]
    unnamed x4 -> x0, starting transfers between devices: 5.84 us -> none
  transfers between devices with their start and end apart: 5 -> 0, of which waited for: 2 -> 0; matrix products, arithmetic and copies ran while one was open for 1% -> 0% of each run, Pallas kernels for 0% -> 0%
where the time goes in v1:
time: 67.6 us; the launch traced here: 67.5 us
  Pallas kernels  63.3 us (94%)
  local copies, waits for them, and re-layouts  3.54 us (5%)
    pallas_call x1, Pallas kernels, local(): pl.pallas_call(kernel, out_shape=(jax.ShapeDtypeStruct((TOK, D), BF16), j...  63.3 us
    unnamed x4, local copies, waits for them, and re-layouts  3.54 us

profile of v1, /device:TPU:1, one launch (start us, length us, event | category | flops | bytes accessed | tf_op | source)
XLA Modules:
  0.0 67.5 jit_solution(3548583023809590910)
XLA Ops:
  0.6 63.3 %step.1 = (bf16[192,4608]{1,0:T(8,128)(2,1)}, f32[504,128]{1,0:T(8,128)}) custom-call(bf16[1,192,448]{2,1,0:T(8,128)(2,1)} %hid_h.1, bf16[1,192,4608]{2,1,0:T(8,128)(2,1)} %cot_h.1, f32[504,128]{1,0:T(8,128)} %bitcast.6, bf16[14,4608]{1,0:T(8,128)(2,1)} %bitcast.7, bf16[1,192,448]{2,1,0:T(8,128)(2,1)} %act_h.1, bf16[256,256]{1,0:T(8,128)(2,1)} %constant.10.clone.fwd_h, ...), custom_call_target="tpu_custom_call" | custom-call | tf_op jit(solution)/shard_map/step/pallas_call | solution.py:558
  63.9 0.0 copy-start
  63.9 2.8 %copy.16 = bf16[1,192,4608]{2,1,0:T(8,128)(2,1)} copy(bf16[1,192,4608]{2,1,0:T(8,128)(2,1)} %bitcast.4) | data formatting | bytes 3538944
  66.8 0.0 copy-done
  66.8 0.7 %copy.17 = f32[1,14,1,4608]{3,2,1,0:T(1,128)} copy(f32[1,14,1,4608]{3,2,1,0:T(1,128)S(1)} %bitcast.5) | data formatting | bytes 516096
Async XLA Ops:
  63.9 2.9 %copy-start = (f32[504,128]{1,0:T(8,128)S(1)}, f32[504,128]{1,0:T(8,128)}, u32[]{:S(2)}) copy-start(f32[504,128]{1,0:T(8,128)} %get-tuple-element.5) | copy-start | bytes 774148

commit v2 on v1

v2 whole, which is shorter than its diff:
```python
import math

import jax
import jax.numpy as jnp
import numpy as np
from jax import lax
from jax.experimental import pallas as pl
from jax.experimental.pallas import tpu as pltpu
from jax.sharding import PartitionSpec as P

SPAN = 256
KEEP = 32
HIGH = SPAN - KEEP
TOK = 192
ROWS = 448
D = 4608
BLOCKS = D // SPAN
OWN = 14
HALF = 224
NY, NZ, NX = 8, 8, 4
SLICE = D // 4
LOW_AT = 4096
CT = LOW_AT + 640
NORM = 1.0 / math.sqrt(TOK * 32)
F32, BF16 = jnp.float32, jnp.bfloat16
HI = lax.Precision.HIGHEST


def tables():
    k = np.arange(SPAN, dtype=np.float64)[:, None]
    n = np.arange(SPAN, dtype=np.float64)[None, :]
    dct = np.cos(np.pi * (2.0 * n + 1.0) * k / (2.0 * SPAN)) * np.sqrt(2.0 / SPAN)
    dct[0] *= np.sqrt(0.5)
    low, high = dct[:KEEP], dct[KEEP:]
    forward = np.concatenate([high, low], axis=0).T
    back = np.concatenate([high, np.zeros((KEEP, SPAN))], axis=0)
    low_t = np.tile(low.T, (1, 4))
    diag = np.zeros((128, 1024))
    for i in range(4):
        diag[32 * i : 32 * i + 32, 256 * i : 256 * i + 256] = low
    diag = np.concatenate([diag, diag], axis=0)
    return (
        jnp.asarray(forward, BF16),
        jnp.asarray(back, BF16),
        jnp.asarray(low_t, F32),
        jnp.asarray(low_t, BF16),
        jnp.asarray(low, F32),
        jnp.asarray(diag, BF16),
    )


def dot(a, b, contract=((1,), (0,)), precision=None):
    return lax.dot_general(
        a, b, (contract, ((), ())), precision=precision, preferred_element_type=F32
    )


def iota(shape, dim):
    return lax.broadcasted_iota(jnp.int32, shape, dim)


def over14(i):
    return (i * 4682) >> 16


FOUND = ((0,), (-1, 1), (-2, 2), (-3, 3), (-4,))
UP = (0, -1, -2, -3)
NEAR = 2


def slot_of(o):
    return o + 4


def hops(d, s):
    return 4 if (s < 2) == (d == 0) else 3


def kernel(
    hid_h, cot_h, mom_h, w_h, act_h, fwd_h, back_h, lowt_h, lowtb_h, low_h, diag_h,
    acc, pair_ref, nm2, diag,
    cot, hid, acts, mom, wraw, fwd, back, lowt, lowtb, low,
    ct, sel, lhs, gram, parts, ring, xs, xr, keep, m2, high8,
    wsh, wx, wbuf, cbuf, cxr, cx, czr, cz, cyr, mbuf, call, actw, actc,
    lsem, hid_s, ct_s, ring_s, x2_s, w0_s, wy_s, wza_s, wzb_s, wzf_s, wxx_s, wsib_s,
    c1_s, c2_s, c3_s, c4_s, c5_s, c6_s,
):
    rep, f = lax.axis_index("rep"), lax.axis_index("fsdp")
    xlo, z = rep // NZ, rep % NZ
    y, xhi, c = f // 4, (f // 2) % 2, f % 2
    x = xhi * 2 + xlo

    def dev(dx=0, dy=0, dz=0, dc=0):
        xx, yy, zz, cc = (x + dx + NX) % NX, (y + dy + NY) % NY, (z + dz + NZ) % NZ, (c + dc) % 2
        return ((xx % 2) * NZ + zz, (yy * 2 + xx // 2) * 2 + cc)

    pending = []

    def send(src, dst, sems, index, to):
        copy = pltpu.make_async_remote_copy(
            src_ref=src, dst_ref=dst, send_sem=sems.at[(0,) + index], recv_sem=sems.at[(1,) + index],
            device_id=to, device_id_type=pl.DeviceIdType.MESH,
        )
        copy.start()
        pending.append(copy)

    def wait(dst, sems, index):
        pltpu.make_async_remote_copy(
            src_ref=dst, dst_ref=dst, send_sem=sems.at[(0,) + index], recv_sem=sems.at[(1,) + index],
            device_id=dev(dc=1), device_id_type=pl.DeviceIdType.MESH,
        ).wait_recv()

    loads = {}
    for i, (name, src, dst) in enumerate((
        ("w", w_h, wraw), ("hid", hid_h.at[0], hid.at[pl.ds(0, TOK)]), ("lowtb", lowtb_h, lowtb),
        ("cot", cot_h.at[0], cot), ("fwd", fwd_h, fwd), ("mom", mom_h, mom), ("lowt", lowt_h, lowt),
        ("low", low_h, low), ("acts", act_h.at[0], acts), ("back", back_h, back), ("diag", diag_h, diag),
    )):
        loads[name] = pltpu.make_async_copy(src, dst, lsem.at[i])
        loads[name].start()

    barrier = pltpu.get_barrier_semaphore()
    friends = [dev(dc=1)]
    friends += [dev(dx=i) for i in range(1, NX)]
    friends += [dev(dy=i) for i in range(1, NY)]
    friends += [dev(dz=i) for i in range(1, NZ)]
    for friend in friends:
        pl.semaphore_signal(barrier, inc=1, device_id=friend, device_id_type=pl.DeviceIdType.MESH)

    i = iota((736, 1), 0)
    w = jnp.where(i < 256, i % 32, i % 32 - 4)
    k = jnp.where(i < 512, 28 * ((i % 256) // 32) + w, i - 512)
    good = (i >= 512) | ((w >= 0) & (w < 28))
    target = jnp.where(good, k + 14 * over14(jnp.maximum(k, 0)) + 14 * c, -1)
    sel[...] = jnp.where(iota((736, ROWS), 1) == target, 1.0, 0.0).astype(BF16)

    loads["w"].wait()
    wsh[...] = jnp.concatenate([wraw[...], jnp.zeros((2, D), BF16)], axis=0)
    loads["hid"].wait()
    pl.semaphore_wait(barrier, len(friends))

    sig = z % 4
    kap = xlo

    def cols(s):
        return pl.ds(pl.multiple_of(((s + 4) % 4) * SLICE, 128), SLICE)

    def wslice(o, s):
        return wbuf.at[c, kap, (y + o + NY) % NY, :, cols(s)]

    def wfull(o, k, core=None):
        return wbuf.at[c if core is None else core, k, (y + o + NY) % NY]

    cross = lax.rem(x + 3 * (1 - xlo) + xlo, NX)
    cross_dev = ((cross % 2) * NZ + z, (y * 2 + cross // 2) * 2 + c)
    send(wsh.at[:, cols(sig)], wx, w0_s, (0,), cross_dev)
    send(hid.at[pl.ds(0, TOK)], hid.at[pl.ds(TOK, TOK)], hid_s, (0,), dev(dc=1))

    loads["lowtb"].wait()
    loads["cot"].wait()
    lane = iota((TOK, 128), 1)
    low_table = lowtb[...]
    for u in range(5):
        tile = jnp.zeros((TOK, 128), F32)
        for i in range(4):
            b = 4 * u + i
            if b < BLOCKS:
                value = dot(cot[:, pl.ds(SPAN * b, SPAN)], low_table)
                tile = jnp.where((lane >= 32 * i) & (lane < 32 * i + 32), value, tile)
        ct[pl.ds(0, TOK), pl.ds(LOW_AT + 128 * u, 128)] = tile.astype(BF16)
    part = pl.ds(LOW_AT, 640)
    send(ct.at[pl.ds(0, TOK), part], ct.at[pl.ds(TOK, TOK), part], ct_s, (4,), dev(dc=1))

    loads["fwd"].wait()
    table = fwd[...]
    for h in range(2):
        high8[h] = dot(cot[:, pl.ds(SPAN * (9 * h + 8), SPAN)], table)
    for s in range(4):
        for q in range(4):
            h, j = q // 2, 4 * (q % 2) + s
            full = dot(cot[:, pl.ds(SPAN * (9 * h + j), SPAN)], table)
            if j < 7:
                extra = high8[h, :, pl.ds(128 * (j // 4), 128)]
                shift = (96 - 32 * (j % 4)) % 128
                extra = pltpu.roll(extra, shift, 1) if shift else extra
            else:
                extra = jnp.zeros((TOK, 128), F32)
            at = 1024 * s + 256 * q
            ct[pl.ds(0, TOK), pl.ds(at, 128)] = full[:, :128].astype(BF16)
            ct[pl.ds(0, TOK), pl.ds(at + 128, 128)] = jnp.where(lane < 96, full[:, 128:], extra).astype(BF16)
        part = pl.ds(1024 * s, 1024)
        send(ct.at[pl.ds(0, TOK), part], ct.at[pl.ds(TOK, TOK), part], ct_s, (s,), dev(dc=1))

    wait(wx, w0_s, (0,))
    own = wsh[:, cols(sig)]
    wslice(0, sig)[...] = jnp.where(jnp.broadcast_to(kap == xhi, own.shape), own, wx[...])

    def wz_send(k):
        for o in FOUND[k]:
            if o:
                wait(wslice(o, sig), wy_s, (slot_of(o),))
            send(wslice(o, sig), wslice(o, sig), wza_s, (slot_of(o),), dev(dz=1))
            send(wslice(o, sig), wslice(o, sig), wzb_s, (slot_of(o),), dev(dz=-1))
            if k < NEAR:
                send(wslice(o, sig), wslice(o, sig), wzf_s, (slot_of(o),), dev(dz=2 if o in UP else -2))

    def wz_pass(k):
        for o in FOUND[k]:
            wait(wslice(o, sig - 1), wza_s, (slot_of(o),))
            wait(wslice(o, sig + 1), wzb_s, (slot_of(o),))
            if k < NEAR:
                continue
            if o in UP:
                send(wslice(o, sig - 1), wslice(o, sig - 1), wzf_s, (slot_of(o),), dev(dz=1))
            else:
                send(wslice(o, sig + 1), wslice(o, sig + 1), wzf_s, (slot_of(o),), dev(dz=-1))

    def wx_send(k):
        for o in FOUND[k]:
            wait(wslice(o, sig + 2), wzf_s, (slot_of(o),))
            send(wfull(o, kap), wfull(o, kap), wxx_s, (slot_of(o),), dev(dx=1 if o in UP else -1))
            send(wfull(o, kap), wfull(o, kap), wsib_s, (0, slot_of(o)), dev(dc=1))

    def wx_wait(k):
        for o in FOUND[k]:
            wait(wfull(o, 1 - kap), wxx_s, (slot_of(o),))
            send(wfull(o, 1 - kap), wfull(o, 1 - kap), wsib_s, (1, slot_of(o)), dev(dc=1))

    def wsib_wait(k):
        for o in FOUND[k]:
            wait(wfull(o, kap, 1 - c), wsib_s, (0, slot_of(o)))
            wait(wfull(o, 1 - kap, 1 - c), wsib_s, (1, slot_of(o)))

    for i in (1, -1, 2, -2, 3, -3, 4):
        o = -i
        send(wslice(0, sig), wslice(0, sig), wy_s, (slot_of(o),), dev(dy=i))
    wz_send(0)

    wait(hid.at[pl.ds(TOK, TOK)], hid_s, (0,))
    lhs[...] = dot(sel[...], hid[...], ((1,), (1,))).astype(BF16)
    left = [lhs[pl.ds(256 * i, 256)] for i in range(2)]

    m2[...] = jnp.zeros_like(m2)
    loads["mom"].wait()
    for b in range(BLOCKS):
        for h in range(2):
            m2[pl.ds(16 * b, OWN), pl.ds(128 * h, 128)] = mom[pl.ds(2 * b + h, OWN, stride=36), :]
    loads["lowt"].wait()
    lane16 = iota((16, 128), 1)
    kept = dot(m2[...], lowt[...], precision=HI)
    tiles = []
    for u in range(5):
        tile = jnp.zeros((16, 128), F32)
        for i in range(4):
            b = 4 * u + i
            if b < BLOCKS:
                good = (lane16 >= 32 * i) & (lane16 < 32 * i + 32)
                tile = jnp.where(good, 0.9 * kept[16 * b : 16 * b + 16], tile)
        tiles.append(tile)
    spread = jnp.concatenate(tiles, axis=1)
    row, col = iota((HALF, 16), 0), iota((HALF, 16), 1)
    place = jnp.where((row == OWN * (2 * y + xhi) + col) & (col < OWN), 1.0, 0.0).astype(BF16)
    spread_top = spread.astype(BF16)
    placed = dot(place, spread_top) + dot(place, (spread - spread_top.astype(F32)).astype(BF16))
    wait(ct.at[pl.ds(TOK, TOK), pl.ds(LOW_AT, 640)], ct_s, (4,))
    local = dot(lhs[pl.ds(512, HALF)], ct[:, pl.ds(LOW_AT, 640)]) * NORM + placed
    for rt in range(14):
        for u in range(4):
            cbuf[4 * rt + u] = local[16 * rt : 16 * rt + 16, 128 * u : 128 * u + 128].astype(BF16)
    for i in range(7):
        a = local[32 * i : 32 * i + 16, 512:640]
        b = local[32 * i + 16 : 32 * i + 32, 512:640]
        cbuf[56 + i] = jnp.where(lane16 < 64, a, pltpu.roll(b, 64, 1)).astype(BF16)
    cbuf[63] = jnp.zeros((16, 128), BF16)

    def c1_send():
        for i in (1, 3, 2):
            to = (x + i) % NX
            send(cbuf.at[pl.ds(16 * to, 16)], cxr.at[i - 1], c1_s, (i - 1,), dev(dx=i))

    def c2_send():
        total = cbuf[pl.ds(16 * x, 16)].astype(F32)
        for i in (1, 3, 2):
            wait(cxr.at[i - 1], c1_s, (i - 1,))
            total = total + cxr[i - 1].astype(F32)
        cx[...] = total.astype(BF16)
        for i in range(1, NZ):
            send(cx.at[pl.ds(2 * ((z + i) % NZ), 2)], czr.at[i - 1], c2_s, (i - 1,), dev(dz=i))

    def c3_send():
        total = cx[pl.ds(2 * z, 2)].astype(F32)
        for i in range(1, NZ):
            wait(czr.at[i - 1], c2_s, (i - 1,))
            total = total + czr[i - 1].astype(F32)
        cz[...] = total.astype(BF16)
        for i in range(1, NY):
            send(cz, cyr.at[i - 1], c3_s, (i - 1,), dev(dy=i))

    def piece(zz):
        return mbuf.at[c, pl.ds(16 * x + 2 * ((zz + NZ) % NZ), 2)]

    def c4_send():
        total = cz[...].astype(F32)
        for i in range(1, NY):
            wait(cyr.at[i - 1], c3_s, (i - 1,))
            total = total + cyr[i - 1].astype(F32)
        piece(z)[...] = (total * (1.0 / 16.0)).astype(BF16)
        for i in range(1, NZ):
            send(piece(z), piece(z), c4_s, (i - 1,), dev(dz=i))

    def strip(xx, core):
        return mbuf.at[core, pl.ds(16 * ((xx + NX) % NX), 16)]

    def c5_send():
        for i in range(1, NZ):
            wait(piece(z - i), c4_s, (i - 1,))
        for i in (1, 3, 2):
            send(strip(x, c), strip(x, c), c5_s, (i - 1,), dev(dx=i))
        send(strip(x, c), strip(x, c), c6_s, (0,), dev(dc=1))

    def c6_send():
        for i in (1, 3, 2):
            wait(strip(x - i, c), c5_s, (i - 1,))
            send(strip(x - i, c), strip(x - i, c), c6_s, (i,), dev(dc=1))

    def c_done():
        for i in range(NX):
            wait(strip(x - i, 1 - c), c6_s, (i,))

    c1_send()

    def towards(d, steps):
        return (y + (steps if d == 0 else -steps) + NY) % NY

    def first_hop(s):
        wait(ct.at[pl.ds(TOK, TOK), pl.ds(1024 * s, 1024)], ct_s, (s,))
        for q in range(4):
            gram[pl.ds(256 * q, 256)] = dot(left[q % 2], ct[:, pl.ds(1024 * s + 256 * q, 256)]) * NORM
        for g in range(NY):
            pieces = []
            for pair in range(2):
                a = gram[pl.ds(512 * pair + 32 * g, 32)]
                b = gram[pl.ds(512 * pair + 256 + 32 * g, 32)]
                pieces += [a[:24], a[24:] + b[:8], b[8:]]
            parts[s, g] = jnp.concatenate(pieces, axis=0).astype(BF16)
        for d in range(2):
            send(parts.at[s, towards(d, hops(d, s))], ring.at[d, s, 0], ring_s, (d, s, 0), dev(dy=1 - 2 * d))

    def next_hop(d, s, k):
        wait(ring.at[d, s, k - 1], ring_s, (d, s, k - 1))
        left_over = hops(d, s) - k
        if left_over:
            total = ring[d, s, k - 1].astype(F32) + parts[s, towards(d, left_over)].astype(F32)
            ring[d, s, k - 1] = total.astype(BF16)
            send(ring.at[d, s, k - 1], ring.at[d, s, k], ring_s, (d, s, k), dev(dy=1 - 2 * d))

    row, col = iota((64, 112), 0), iota((64, 112), 1)
    j, q16 = row % 16, row // 16

    def pick_rows(hi):
        return jnp.where((j < OWN) & (col == 28 * q16 + 14 * hi + j), 1.0, 0.0).astype(BF16)

    theirs, ours = pick_rows(1 - xhi), pick_rows(xhi)

    def exchange(s):
        total = parts[s, y].astype(F32)
        for d in range(2):
            total = total + ring[d, s, hops(d, s) - 1].astype(F32)
        chunk = total.astype(BF16)
        xs[s] = dot(theirs, chunk).astype(BF16)
        send(xs.at[s], xr.at[s], x2_s, (s,), dev(dx=2))
        keep[s] = dot(ours, chunk)

    def momentum_rest():
        loads["low"].wait()
        nm2[...] = 0.9 * (m2[...] - dot(kept[:, :KEEP], low[...], precision=HI))

    def left_two():
        loads["acts"].wait()
        a = acts[...]
        for core in range(2):
            i = iota((1, HALF), 1)
            target = i + 14 * over14(i) + 14 * core
            pick = jnp.where(iota((ROWS, HALF), 0) == target, 1.0, 0.0)
            actc[core] = dot(a, pick.astype(BF16)).astype(BF16)
            i = iota((1, 256), 1)
            j, t = i % 16, i // 16
            target = jnp.where(j < OWN, 56 * (t % 8) + 28 * (t // 8) + 14 * core + j, -1)
            pick = jnp.where(iota((ROWS, 256), 0) == target, 1.0, 0.0)
            actw[:, pl.ds(256 * core, 256)] = dot(a, pick.astype(BF16)).astype(BF16)

    for s in range(4):
        first_hop(s)

    events = [
        (8.0, momentum_rest, ()),
        (8.1, left_two, ()),
        (9, wz_pass, (0,)),
        (9.2, wz_send, (1,)),
        (10.7, wz_send, (2,)),
        (11.5, c2_send, ()),
        (11.6, wx_send, (0,)),
        (12.2, wz_send, (3,)),
        (12.3, wz_pass, (1,)),
        (13.5, wz_send, (4,)),
        (13.7, wz_pass, (2,)),
        (12.4, wx_send, (1,)),
        (16, c3_send, ()),
        (16.05, wz_pass, (3,)),
        (17, wz_pass, (4,)),
        (17.1, wx_send, (2,)),
        (16, wx_wait, (0,)),
        (19.5, wx_send, (3,)),
        (18.5, wx_wait, (1,)),
        (20.5, c4_send, ()),
        (21, wx_send, (4,)),
        (23, wx_wait, (2,)),
        (25, c5_send, ()),
        (26, wx_wait, (3,)),
        (27.5, wx_wait, (4,)),
        (29.5, c6_send, ()),
    ]
    at = 12
    for k in range(1, 5):
        for s in range(4):
            for d in range(2):
                if k <= hops(d, s):
                    events.append((at, next_hop, (d, s, k)))
            at += 1.4
    for s in range(4):
        events.append((at + 0.01 * s, exchange, (s,)))
    events.sort(key=lambda event: event[0])
    for _, run, given in events:
        run(*given)

    for k in range(5):
        wsib_wait(k)
    for t in range(4):
        at = pl.ds(SLICE * t, SLICE)
        acc[:, at] = dot(actw[...], wbuf[:, :, :, :, at].reshape(512, SLICE))
    loads["back"].wait()
    inverse = back[...]
    eights = [[jnp.zeros((16, 128), F32) for _ in range(2)] for _ in range(2)]

    def to_space(values):
        big = values.astype(BF16)
        return dot(big, inverse) + dot((values - big.astype(F32)).astype(BF16), inverse)

    for s in range(4):
        wait(xr.at[s], x2_s, (s,))
        total = keep[s] + xr[s].astype(F32)
        space = to_space(total)
        for q in range(4):
            h, j = q // 2, 4 * (q % 2) + s
            at = pl.ds(16 * (9 * h + j), 16)
            nm2[at] = nm2[at] + space[16 * q : 16 * q + 16]
            if j < 7:
                tail = total[16 * q : 16 * q + 16, 128:]
                spot = 32 * (j % 4)
                tail = pltpu.roll(tail, (spot - 96) % 128, 1) if spot != 96 else tail
                good = (lane16 >= spot) & (lane16 < spot + 32)
                eights[h][j // 4] = jnp.where(good, tail, eights[h][j // 4])
    for h in range(2):
        at = pl.ds(16 * (9 * h + 8), 16)
        nm2[at] = nm2[at] + to_space(jnp.concatenate(eights[h], axis=1))

    c_done()
    for core in range(2):
        for rt in range(14):
            for u in range(4):
                call[pl.ds(HALF * core + 16 * rt, 16), pl.ds(128 * u, 128)] = mbuf[core, 4 * rt + u]
        for i in range(7):
            tile = mbuf[core, 56 + i].astype(F32)
            at = HALF * core + 32 * i
            call[pl.ds(at, 16), pl.ds(512, 128)] = jnp.where(lane16 < 64, tile, 0.0).astype(BF16)
            call[pl.ds(at + 16, 16), pl.ds(512, 128)] = jnp.where(
                lane16 < 64, pltpu.roll(tile, 64, 1), 0.0
            ).astype(BF16)
    inner = dot(actc[0], call[pl.ds(0, HALF)]) + dot(actc[1], call[pl.ds(HALF, HALF)])
    inner = inner * 0.5
    top = inner.astype(BF16)
    rest = (inner - top.astype(F32)).astype(BF16)
    for u in range(5):
        pair_ref[:, pl.ds(256 * u, 128)] = top[:, 128 * u : 128 * u + 128]
        pair_ref[:, pl.ds(256 * u + 128, 128)] = rest[:, 128 * u : 128 * u + 128]

    loads["diag"].wait()
    for copy in pending:
        copy.wait_send()


def finish(acc, pair, nm2, diag, out_h, nm_h, out, nm, sems):
    copies = []
    for u in range(5):
        width = 1024 if u < 4 else 512
        at = pl.ds(1024 * u, width)
        out[:, at] = (acc[:, at] - dot(pair[:, pl.ds(256 * u, 256)], diag[:, pl.ds(0, width)])).astype(BF16)
        copies.append(pltpu.make_async_copy(out.at[:, at], out_h.at[:, at], sems.at[u]))
        copies[-1].start()
    for b in range(BLOCKS):
        for h in range(2):
            nm[pl.ds(2 * b + h, OWN, stride=36), :] = nm2[pl.ds(16 * b, OWN), pl.ds(128 * h, 128)]
    copies.append(pltpu.make_async_copy(nm, nm_h, sems.at[5]))
    copies[-1].start()
    for copy in copies:
        copy.wait()


def local(hid_acts, out_cot, momentum, weight, next_acts):
    any_space = pl.BlockSpec(memory_space=pl.ANY)
    hbm = pl.BlockSpec(memory_space=pltpu.HBM)
    vmem = pl.BlockSpec(memory_space=pltpu.VMEM)
    dma = pltpu.SemaphoreType.DMA
    scratch = [
        pltpu.VMEM((TOK, D), BF16),
        pltpu.VMEM((2 * TOK, ROWS), BF16),
        pltpu.VMEM((TOK, ROWS), BF16),
        pltpu.VMEM((504, 128), F32),
        pltpu.VMEM((OWN, D), BF16),
        pltpu.VMEM((SPAN, SPAN), BF16),
        pltpu.VMEM((SPAN, SPAN), BF16),
        pltpu.VMEM((SPAN, 128), F32),
        pltpu.VMEM((SPAN, 128), BF16),
        pltpu.VMEM((KEEP, SPAN), F32),
        pltpu.VMEM((2 * TOK, CT), BF16),
        pltpu.VMEM((736, ROWS), BF16),
        pltpu.VMEM((736, 2 * TOK), BF16),
        pltpu.VMEM((1024, 256), F32),
        pltpu.VMEM((4, NY, 112, 256), BF16),
        pltpu.VMEM((2, 4, 4, 112, 256), BF16),
        pltpu.VMEM((4, 64, 256), BF16),
        pltpu.VMEM((4, 64, 256), BF16),
        pltpu.VMEM((4, 64, 256), F32),
        pltpu.VMEM((16 * BLOCKS, SPAN), F32),
        pltpu.VMEM((2, TOK, SPAN), F32),
        pltpu.VMEM((16, D), BF16),
        pltpu.VMEM((16, SLICE), BF16),
        pltpu.VMEM((2, 2, NY, 16, D), BF16),
        pltpu.VMEM((64, 16, 128), BF16),
        pltpu.VMEM((3, 16, 16, 128), BF16),
        pltpu.VMEM((16, 16, 128), BF16),
        pltpu.VMEM((7, 2, 16, 128), BF16),
        pltpu.VMEM((2, 16, 128), BF16),
        pltpu.VMEM((7, 2, 16, 128), BF16),
        pltpu.VMEM((2, 64, 16, 128), BF16),
        pltpu.VMEM((ROWS, 640), BF16),
        pltpu.VMEM((TOK, 512), BF16),
        pltpu.VMEM((2, TOK, HALF), BF16),
        dma((11,)),
        dma((2, 1)),
        dma((2, 5)),
        dma((2, 2, 4, 4)),
        dma((2, 4)),
        dma((2, 1)),
        dma((2, 8)),
        dma((2, 8)),
        dma((2, 8)),
        dma((2, 8)),
        dma((2, 8)),
        dma((2, 2, 8)),
        dma((2, 3)),
        dma((2, 7)),
        dma((2, 7)),
        dma((2, 7)),
        dma((2, 3)),
        dma((2, 4)),
    ]
    given = (
        hid_acts,
        out_cot,
        momentum.reshape(504, 128),
        weight.reshape(OWN, D),
        next_acts,
        *tables(),
    )
    held = pl.pallas_call(
        kernel,
        out_shape=(
            pltpu.VMEM((TOK, D), F32),
            pltpu.VMEM((TOK, 5 * SPAN), BF16),
            pltpu.VMEM((16 * BLOCKS, SPAN), F32),
            pltpu.VMEM((SPAN, 1024), BF16),
        ),
        in_specs=[hbm] * 11,
        out_specs=(vmem,) * 4,
        scratch_shapes=scratch,
        compiler_params=pltpu.CompilerParams(
            collective_id=0, has_side_effects=True, vmem_limit_bytes=40 * 2**20
        ),
        name="step",
    )(
        *(pltpu.with_memory_space_constraint(a, pltpu.HBM) for a in given)
    )
    held = [pltpu.with_memory_space_constraint(a, pltpu.VMEM) for a in held]
    out, nm = pl.pallas_call(
        finish,
        out_shape=(
            jax.ShapeDtypeStruct((TOK, D), BF16),
            jax.ShapeDtypeStruct((504, 128), F32),
        ),
        in_specs=[vmem] * 4,
        out_specs=(any_space, any_space),
        scratch_shapes=[pltpu.VMEM((TOK, D), BF16), pltpu.VMEM((504, 128), F32), dma((6,))],
        compiler_params=pltpu.CompilerParams(vmem_limit_bytes=8 * 2**20),
        name="finish",
    )(*held)
    return out[None], nm.reshape(1, OWN, 1, D)


def solution(mesh):
    return jax.shard_map(
        local,
        mesh=mesh,
        in_specs=(
            P(None, ("rep", "fsdp"), None),
            P(None, ("rep", "fsdp"), None),
            P("rep", "fsdp", None, None),
            P("fsdp", None, None),
            P(None, ("rep", "fsdp"), None),
        ),
        out_specs=(P(None, ("rep", "fsdp"), None), P("rep", "fsdp", None, None)),
        check_vma=False,
    )
```

time: 67.6 us -> 59.4 us (0.88)
  the two profiles are of different devices: /device:TPU:1 before, /device:TPU:2 now
where the time goes in v2:
time: 59.4 us; the launch traced here: 59.3 us
  Pallas kernels  58.7 us (99%)
  between operations  0.64 us (1%)
    pallas_call x1, Pallas kernels, local(): pl.pallas_call(kernel, out_shape=(pltpu.VMEM((TOK, D), F32), pltpu.VMEM((...  57.1 us
    pallas_call x1, Pallas kernels, local(): pl.pallas_call(finish, out_shape=(jax.ShapeDtypeStruct((TOK, D), BF16), j...  1.61 us

profile of v2, /device:TPU:2, one launch (start us, length us, event | category | flops | bytes accessed | tf_op | source)
XLA Modules:
  0.0 59.3 jit_solution(1931230128699334165)
XLA Ops:
  0.6 57.1 %step.1 = (f32[192,4608]{1,0:T(8,128)S(1)}, bf16[192,1280]{1,0:T(8,128)(2,1)S(1)}, f32[288,256]{1,0:T(8,128)S(1)}, bf16[256,1024]{1,0:T(8,128)(2,1)S(1)}) custom-call(bf16[1,192,448]{2,1,0:T(8,128)(2,1)} %hid_h.1, bf16[1,192,4608]{2,1,0:T(8,128)(2,1)} %cot_h.1, f32[504,128]{1,0:T(8,128)} %bitcast.4, bf16[14,4608]{1,0:T(8,128)(2,1)} %bitcast.5, ...), custom_call_target="tpu_custom_call" | custom-call | tf_op jit(solution)/shard_map/step/pallas_call | solution.py:576
  57.7 1.6 %finish.1 = (bf16[192,4608]{1,0:T(8,128)(2,1)}, f32[504,128]{1,0:T(8,128)}) custom-call(f32[192,4608]{1,0:T(8,128)S(1)} %get-tuple-element.8.acc, bf16[192,1280]{1,0:T(8,128)(2,1)S(1)} %get-tuple-element.9.pair, f32[288,256]{1,0:T(8,128)S(1)} %get-tuple-element.10.nm2, bf16[256,1024]{1,0:T(8,128)(2,1)S(1)} %get-tuple-element.11.diag), custom_call_target="tpu_custom_call" | custom-call | tf_op jit(solution)/shard_map/finish/pallas_call | solution.py:595

commit v3 on v2

--- a/solution.py
+++ b/solution.py
@@ -199,6 +199,9 @@
         for o in FOUND[k]:
             if o:
                 wait(wslice(o, sig), wy_s, (slot_of(o),))
+            if o in (-2, 2, -3):
+                step = 1 if o < 0 else -1
+                send(wslice(o, sig), wslice(o, sig), wy_s, (slot_of(o - step),), dev(dy=step))
             send(wslice(o, sig), wslice(o, sig), wza_s, (slot_of(o),), dev(dz=1))
             send(wslice(o, sig), wslice(o, sig), wzb_s, (slot_of(o),), dev(dz=-1))
             if k < NEAR:
@@ -231,7 +234,7 @@
             wait(wfull(o, kap, 1 - c), wsib_s, (0, slot_of(o)))
             wait(wfull(o, 1 - kap, 1 - c), wsib_s, (1, slot_of(o)))
 
-    for i in (1, -1, 2, -2, 3, -3, 4):
+    for i in (1, -1, 2, -2):
         o = -i
         send(wslice(0, sig), wslice(0, sig), wy_s, (slot_of(o),), dev(dy=i))
     wz_send(0)
@@ -239,6 +242,34 @@
     wait(hid.at[pl.ds(TOK, TOK)], hid_s, (0,))
     lhs[...] = dot(sel[...], hid[...], ((1,), (1,))).astype(BF16)
     left = [lhs[pl.ds(256 * i, 256)] for i in range(2)]
+
+    def towards(d, steps):
+        return (y + (steps if d == 0 else -steps) + NY) % NY
+
+    def first_hop(s):
+        wait(ct.at[pl.ds(TOK, TOK), pl.ds(1024 * s, 1024)], ct_s, (s,))
+        for q in range(4):
+            gram[pl.ds(256 * q, 256)] = dot(left[q % 2], ct[:, pl.ds(1024 * s + 256 * q, 256)]) * NORM
+        for g in range(NY):
+            pieces = []
+            for pair in range(2):
+                a = gram[pl.ds(512 * pair + 32 * g, 32)]
+                b = gram[pl.ds(512 * pair + 256 + 32 * g, 32)]
+                pieces += [a[:24], a[24:] + b[:8], b[8:]]
+            parts[s, g] = jnp.concatenate(pieces, axis=0).astype(BF16)
+        for d in range(2):
+            send(parts.at[s, towards(d, hops(d, s))], ring.at[d, s, 0], ring_s, (d, s, 0), dev(dy=1 - 2 * d))
+
+    def next_hop(d, s, k):
+        wait(ring.at[d, s, k - 1], ring_s, (d, s, k - 1))
+        left_over = hops(d, s) - k
+        if left_over:
+            total = ring[d, s, k - 1].astype(F32) + parts[s, towards(d, left_over)].astype(F32)
+            ring[d, s, k - 1] = total.astype(BF16)
+            send(ring.at[d, s, k - 1], ring.at[d, s, k], ring_s, (d, s, k), dev(dy=1 - 2 * d))
+
+    for s in range(4):
+        first_hop(s)
 
     m2[...] = jnp.zeros_like(m2)
     loads["mom"].wait()
@@ -329,31 +360,6 @@
 
     c1_send()
 
-    def towards(d, steps):
-        return (y + (steps if d == 0 else -steps) + NY) % NY
-
-    def first_hop(s):
-        wait(ct.at[pl.ds(TOK, TOK), pl.ds(1024 * s, 1024)], ct_s, (s,))
-        for q in range(4):
-            gram[pl.ds(256 * q, 256)] = dot(left[q % 2], ct[:, pl.ds(1024 * s + 256 * q, 256)]) * NORM
-        for g in range(NY):
-            pieces = []
-            for pair in range(2):
-                a = gram[pl.ds(512 * pair + 32 * g, 32)]
-                b = gram[pl.ds(512 * pair + 256 + 32 * g, 32)]
-                pieces += [a[:24], a[24:] + b[:8], b[8:]]
-            parts[s, g] = jnp.concatenate(pieces, axis=0).astype(BF16)
-        for d in range(2):
-            send(parts.at[s, towards(d, hops(d, s))], ring.at[d, s, 0], ring_s, (d, s, 0), dev(dy=1 - 2 * d))
-
-    def next_hop(d, s, k):
-        wait(ring.at[d, s, k - 1], ring_s, (d, s, k - 1))
-        left_over = hops(d, s) - k
-        if left_over:
-            total = ring[d, s, k - 1].astype(F32) + parts[s, towards(d, left_over)].astype(F32)
-            ring[d, s, k - 1] = total.astype(BF16)
-            send(ring.at[d, s, k - 1], ring.at[d, s, k], ring_s, (d, s, k), dev(dy=1 - 2 * d))
-
     row, col = iota((64, 112), 0), iota((64, 112), 1)
     j, q16 = row % 16, row // 16
 
@@ -389,35 +395,33 @@
             pick = jnp.where(iota((ROWS, 256), 0) == target, 1.0, 0.0)
             actw[:, pl.ds(256 * core, 256)] = dot(a, pick.astype(BF16)).astype(BF16)
 
-    for s in range(4):
-        first_hop(s)
 
     events = [
         (8.0, momentum_rest, ()),
         (8.1, left_two, ()),
         (9, wz_pass, (0,)),
-        (9.2, wz_send, (1,)),
-        (10.7, wz_send, (2,)),
+        (8.9, wz_send, (1,)),
+        (10.1, wz_send, (2,)),
         (11.5, c2_send, ()),
         (11.6, wx_send, (0,)),
-        (12.2, wz_send, (3,)),
+        (13.2, wz_send, (3,)),
         (12.3, wz_pass, (1,)),
-        (13.5, wz_send, (4,)),
-        (13.7, wz_pass, (2,)),
+        (16.4, wz_send, (4,)),
+        (13.5, wz_pass, (2,)),
         (12.4, wx_send, (1,)),
         (16, c3_send, ()),
-        (16.05, wz_pass, (3,)),
-        (17, wz_pass, (4,)),
+        (16.6, wz_pass, (3,)),
+        (19.7, wz_pass, (4,)),
         (17.1, wx_send, (2,)),
         (16, wx_wait, (0,)),
-        (19.5, wx_send, (3,)),
+        (20, wx_send, (3,)),
         (18.5, wx_wait, (1,)),
         (20.5, c4_send, ()),
-        (21, wx_send, (4,)),
-        (23, wx_wait, (2,)),
+        (23, wx_send, (4,)),
+        (22, wx_wait, (2,)),
         (25, c5_send, ()),
-        (26, wx_wait, (3,)),
-        (27.5, wx_wait, (4,)),
+        (25.5, wx_wait, (3,)),
+        (28, wx_wait, (4,)),
         (29.5, c6_send, ()),
     ]
     at = 12
@@ -464,19 +468,21 @@
         at = pl.ds(16 * (9 * h + 8), 16)
         nm2[at] = nm2[at] + to_space(jnp.concatenate(eights[h], axis=1))
 
-    c_done()
-    for core in range(2):
+    def kept_part(core, at):
         for rt in range(14):
             for u in range(4):
-                call[pl.ds(HALF * core + 16 * rt, 16), pl.ds(128 * u, 128)] = mbuf[core, 4 * rt + u]
+                call[pl.ds(at + 16 * rt, 16), pl.ds(128 * u, 128)] = mbuf[core, 4 * rt + u]
         for i in range(7):
             tile = mbuf[core, 56 + i].astype(F32)
-            at = HALF * core + 32 * i
-            call[pl.ds(at, 16), pl.ds(512, 128)] = jnp.where(lane16 < 64, tile, 0.0).astype(BF16)
-            call[pl.ds(at + 16, 16), pl.ds(512, 128)] = jnp.where(
+            call[pl.ds(at + 32 * i, 16), pl.ds(512, 128)] = jnp.where(lane16 < 64, tile, 0.0).astype(BF16)
+            call[pl.ds(at + 32 * i + 16, 16), pl.ds(512, 128)] = jnp.where(
                 lane16 < 64, pltpu.roll(tile, 64, 1), 0.0
             ).astype(BF16)
-    inner = dot(actc[0], call[pl.ds(0, HALF)]) + dot(actc[1], call[pl.ds(HALF, HALF)])
+        return dot(actc[core], call[pl.ds(at, HALF)])
+
+    inner = kept_part(c, 0)
+    c_done()
+    inner = inner + kept_part(1 - c, HALF)
     inner = inner * 0.5
     top = inner.astype(BF16)
     rest = (inner - top.astype(F32)).astype(BF16)

time: 59.4 us -> 58.1 us (0.978)
  the two profiles are of different devices: /device:TPU:2 before, /device:TPU:64 now
where the time goes in v3:
time: 58.1 us; the launch traced here: 58 us
  Pallas kernels  57.3 us (99%)
  between operations  0.64 us (1%)
    pallas_call x1, Pallas kernels, local(): pl.pallas_call(kernel, out_shape=(pltpu.VMEM((TOK, D), F32), pltpu.VMEM((...  55.7 us
    pallas_call x1, Pallas kernels, local(): pl.pallas_call(finish, out_shape=(jax.ShapeDtypeStruct((TOK, D), BF16), j...  1.61 us

profile of v3, /device:TPU:64, one launch (start us, length us, event | category | flops | bytes accessed | tf_op | source)
XLA Modules:
  0.0 58.0 jit_solution(2561650073703286346)
XLA Ops:
  0.6 55.7 %step.1 = (f32[192,4608]{1,0:T(8,128)S(1)}, bf16[192,1280]{1,0:T(8,128)(2,1)S(1)}, f32[288,256]{1,0:T(8,128)S(1)}, bf16[256,1024]{1,0:T(8,128)(2,1)S(1)}) custom-call(bf16[1,192,448]{2,1,0:T(8,128)(2,1)} %hid_h.1, bf16[1,192,4608]{2,1,0:T(8,128)(2,1)} %cot_h.1, f32[504,128]{1,0:T(8,128)} %bitcast.4, bf16[14,4608]{1,0:T(8,128)(2,1)} %bitcast.5, ...), custom_call_target="tpu_custom_call" | custom-call | tf_op jit(solution)/shard_map/step/pallas_call | solution.py:582
  56.4 1.6 %finish.1 = (bf16[192,4608]{1,0:T(8,128)(2,1)}, f32[504,128]{1,0:T(8,128)}) custom-call(f32[192,4608]{1,0:T(8,128)S(1)} %get-tuple-element.8.acc, bf16[192,1280]{1,0:T(8,128)(2,1)S(1)} %get-tuple-element.9.pair, f32[288,256]{1,0:T(8,128)S(1)} %get-tuple-element.10.nm2, bf16[256,1024]{1,0:T(8,128)(2,1)S(1)} %get-tuple-element.11.diag), custom_call_target="tpu_custom_call" | custom-call | tf_op jit(solution)/shard_map/finish/pallas_call | solution.py:601

commit v4 on v3

--- a/solution.py
+++ b/solution.py
@@ -190,86 +190,6 @@
             ct[pl.ds(0, TOK), pl.ds(at + 128, 128)] = jnp.where(lane < 96, full[:, 128:], extra).astype(BF16)
         part = pl.ds(1024 * s, 1024)
         send(ct.at[pl.ds(0, TOK), part], ct.at[pl.ds(TOK, TOK), part], ct_s, (s,), dev(dc=1))
-
-    wait(wx, w0_s, (0,))
-    own = wsh[:, cols(sig)]
-    wslice(0, sig)[...] = jnp.where(jnp.broadcast_to(kap == xhi, own.shape), own, wx[...])
-
-    def wz_send(k):
-        for o in FOUND[k]:
-            if o:
-                wait(wslice(o, sig), wy_s, (slot_of(o),))
-            if o in (-2, 2, -3):
-                step = 1 if o < 0 else -1
-                send(wslice(o, sig), wslice(o, sig), wy_s, (slot_of(o - step),), dev(dy=step))
-            send(wslice(o, sig), wslice(o, sig), wza_s, (slot_of(o),), dev(dz=1))
-            send(wslice(o, sig), wslice(o, sig), wzb_s, (slot_of(o),), dev(dz=-1))
-            if k < NEAR:
-                send(wslice(o, sig), wslice(o, sig), wzf_s, (slot_of(o),), dev(dz=2 if o in UP else -2))
-
-    def wz_pass(k):
-        for o in FOUND[k]:
-            wait(wslice(o, sig - 1), wza_s, (slot_of(o),))
-            wait(wslice(o, sig + 1), wzb_s, (slot_of(o),))
-            if k < NEAR:
-                continue
-            if o in UP:
-                send(wslice(o, sig - 1), wslice(o, sig - 1), wzf_s, (slot_of(o),), dev(dz=1))
-            else:
-                send(wslice(o, sig + 1), wslice(o, sig + 1), wzf_s, (slot_of(o),), dev(dz=-1))
-
-    def wx_send(k):
-        for o in FOUND[k]:
-            wait(wslice(o, sig + 2), wzf_s, (slot_of(o),))
-            send(wfull(o, kap), wfull(o, kap), wxx_s, (slot_of(o),), dev(dx=1 if o in UP else -1))
-            send(wfull(o, kap), wfull(o, kap), wsib_s, (0, slot_of(o)), dev(dc=1))
-
-    def wx_wait(k):
-        for o in FOUND[k]:
-            wait(wfull(o, 1 - kap), wxx_s, (slot_of(o),))
-            send(wfull(o, 1 - kap), wfull(o, 1 - kap), wsib_s, (1, slot_of(o)), dev(dc=1))
-
-    def wsib_wait(k):
-        for o in FOUND[k]:
-            wait(wfull(o, kap, 1 - c), wsib_s, (0, slot_of(o)))
-            wait(wfull(o, 1 - kap, 1 - c), wsib_s, (1, slot_of(o)))
-
-    for i in (1, -1, 2, -2):
-        o = -i
-        send(wslice(0, sig), wslice(0, sig), wy_s, (slot_of(o),), dev(dy=i))
-    wz_send(0)
-
-    wait(hid.at[pl.ds(TOK, TOK)], hid_s, (0,))
-    lhs[...] = dot(sel[...], hid[...], ((1,), (1,))).astype(BF16)
-    left = [lhs[pl.ds(256 * i, 256)] for i in range(2)]
-
-    def towards(d, steps):
-        return (y + (steps if d == 0 else -steps) + NY) % NY
-
-    def first_hop(s):
-        wait(ct.at[pl.ds(TOK, TOK), pl.ds(1024 * s, 1024)], ct_s, (s,))
-        for q in range(4):
-            gram[pl.ds(256 * q, 256)] = dot(left[q % 2], ct[:, pl.ds(1024 * s + 256 * q, 256)]) * NORM
-        for g in range(NY):
-            pieces = []
-            for pair in range(2):
-                a = gram[pl.ds(512 * pair + 32 * g, 32)]
-                b = gram[pl.ds(512 * pair + 256 + 32 * g, 32)]
-                pieces += [a[:24], a[24:] + b[:8], b[8:]]
-            parts[s, g] = jnp.concatenate(pieces, axis=0).astype(BF16)
-        for d in range(2):
-            send(parts.at[s, towards(d, hops(d, s))], ring.at[d, s, 0], ring_s, (d, s, 0), dev(dy=1 - 2 * d))
-
-    def next_hop(d, s, k):
-        wait(ring.at[d, s, k - 1], ring_s, (d, s, k - 1))
-        left_over = hops(d, s) - k
-        if left_over:
-            total = ring[d, s, k - 1].astype(F32) + parts[s, towards(d, left_over)].astype(F32)
-            ring[d, s, k - 1] = total.astype(BF16)
-            send(ring.at[d, s, k - 1], ring.at[d, s, k], ring_s, (d, s, k), dev(dy=1 - 2 * d))
-
-    for s in range(4):
-        first_hop(s)
 
     m2[...] = jnp.zeros_like(m2)
     loads["mom"].wait()
@@ -293,6 +213,87 @@
     place = jnp.where((row == OWN * (2 * y + xhi) + col) & (col < OWN), 1.0, 0.0).astype(BF16)
     spread_top = spread.astype(BF16)
     placed = dot(place, spread_top) + dot(place, (spread - spread_top.astype(F32)).astype(BF16))
+
+    wait(wx, w0_s, (0,))
+    own = wsh[:, cols(sig)]
+    wslice(0, sig)[...] = jnp.where(jnp.broadcast_to(kap == xhi, own.shape), own, wx[...])
+
+    def wz_send(k):
+        for o in FOUND[k]:
+            if o:
+                wait(wslice(o, sig), wy_s, (slot_of(o),))
+            if o in (-2, 2, -3):
+                step = 1 if o < 0 else -1
+                send(wslice(o, sig), wslice(o, sig), wy_s, (slot_of(o - step),), dev(dy=step))
+            send(wslice(o, sig), wslice(o, sig), wza_s, (slot_of(o),), dev(dz=1))
+            send(wslice(o, sig), wslice(o, sig), wzb_s, (slot_of(o),), dev(dz=-1))
+            if k < NEAR:
+                send(wslice(o, sig), wslice(o, sig), wzf_s, (slot_of(o),), dev(dz=2 if o in UP else -2))
+
+    def wz_pass(k):
+        for o in FOUND[k]:
+            wait(wslice(o, sig - 1), wza_s, (slot_of(o),))
+            wait(wslice(o, sig + 1), wzb_s, (slot_of(o),))
+            if k < NEAR:
+                continue
+            if o in UP:
+                send(wslice(o, sig - 1), wslice(o, sig - 1), wzf_s, (slot_of(o),), dev(dz=1))
+            else:
+                send(wslice(o, sig + 1), wslice(o, sig + 1), wzf_s, (slot_of(o),), dev(dz=-1))
+
+    def wx_send(k):
+        for o in FOUND[k]:
+            wait(wslice(o, sig + 2), wzf_s, (slot_of(o),))
+            send(wfull(o, kap), wfull(o, kap), wxx_s, (slot_of(o),), dev(dx=1 if o in UP else -1))
+            send(wfull(o, kap), wfull(o, kap), wsib_s, (0, slot_of(o)), dev(dc=1))
+
+    def wx_wait(k):
+        for o in FOUND[k]:
+            wait(wfull(o, 1 - kap), wxx_s, (slot_of(o),))
+            send(wfull(o, 1 - kap), wfull(o, 1 - kap), wsib_s, (1, slot_of(o)), dev(dc=1))
+
+    def wsib_wait(k):
+        for o in FOUND[k]:
+            wait(wfull(o, kap, 1 - c), wsib_s, (0, slot_of(o)))
+            wait(wfull(o, 1 - kap, 1 - c), wsib_s, (1, slot_of(o)))
+
+    for i in (1, -1, 2, -2):
+        o = -i
+        send(wslice(0, sig), wslice(0, sig), wy_s, (slot_of(o),), dev(dy=i))
+    wz_send(0)
+
+    wait(hid.at[pl.ds(TOK, TOK)], hid_s, (0,))
+    lhs[...] = dot(sel[...], hid[...], ((1,), (1,))).astype(BF16)
+    left = [lhs[pl.ds(256 * i, 256)] for i in range(2)]
+
+    def towards(d, steps):
+        return (y + (steps if d == 0 else -steps) + NY) % NY
+
+    def first_hop(s):
+        wait(ct.at[pl.ds(TOK, TOK), pl.ds(1024 * s, 1024)], ct_s, (s,))
+        for q in range(4):
+            gram[pl.ds(256 * q, 256)] = dot(left[q % 2], ct[:, pl.ds(1024 * s + 256 * q, 256)]) * NORM
+        for g in range(NY):
+            pieces = []
+            for pair in range(2):
+                a = gram[pl.ds(512 * pair + 32 * g, 32)]
+                b = gram[pl.ds(512 * pair + 256 + 32 * g, 32)]
+                pieces += [a[:24], a[24:] + b[:8], b[8:]]
+            parts[s, g] = jnp.concatenate(pieces, axis=0).astype(BF16)
+        for d in range(2):
+            send(parts.at[s, towards(d, hops(d, s))], ring.at[d, s, 0], ring_s, (d, s, 0), dev(dy=1 - 2 * d))
+
+    def next_hop(d, s, k):
+        wait(ring.at[d, s, k - 1], ring_s, (d, s, k - 1))
+        left_over = hops(d, s) - k
+        if left_over:
+            total = ring[d, s, k - 1].astype(F32) + parts[s, towards(d, left_over)].astype(F32)
+            ring[d, s, k - 1] = total.astype(BF16)
+            send(ring.at[d, s, k - 1], ring.at[d, s, k], ring_s, (d, s, k), dev(dy=1 - 2 * d))
+
+    for s in range(4):
+        first_hop(s)
+
     wait(ct.at[pl.ds(TOK, TOK), pl.ds(LOW_AT, 640)], ct_s, (4,))
     local = dot(lhs[pl.ds(512, HALF)], ct[:, pl.ds(LOW_AT, 640)]) * NORM + placed
     for rt in range(14):

time: 58.1 us -> 57.1 us (0.983)
  the two profiles are of different devices: /device:TPU:64 before, /device:TPU:8 now
where the time goes in v4:
time: 57.1 us; the launch traced here: 57 us
  Pallas kernels  56.3 us (99%)
  between operations  0.64 us (1%)
    pallas_call x1, Pallas kernels, local(): pl.pallas_call(kernel, out_shape=(pltpu.VMEM((TOK, D), F32), pltpu.VMEM((...  54.7 us
    pallas_call x1, Pallas kernels, local(): pl.pallas_call(finish, out_shape=(jax.ShapeDtypeStruct((TOK, D), BF16), j...  1.61 us

profile of v4, /device:TPU:8, one launch (start us, length us, event | category | flops | bytes accessed | tf_op | source)
XLA Modules:
  0.0 57.0 jit_solution(5907768669095197942)
XLA Ops:
  0.6 54.7 %step.1 = (f32[192,4608]{1,0:T(8,128)S(1)}, bf16[192,1280]{1,0:T(8,128)(2,1)S(1)}, f32[288,256]{1,0:T(8,128)S(1)}, bf16[256,1024]{1,0:T(8,128)(2,1)S(1)}) custom-call(bf16[1,192,448]{2,1,0:T(8,128)(2,1)} %hid_h.1, bf16[1,192,4608]{2,1,0:T(8,128)(2,1)} %cot_h.1, f32[504,128]{1,0:T(8,128)} %bitcast.4, bf16[14,4608]{1,0:T(8,128)(2,1)} %bitcast.5, ...), custom_call_target="tpu_custom_call" | custom-call | tf_op jit(solution)/shard_map/step/pallas_call | solution.py:583
  55.4 1.6 %finish.1 = (bf16[192,4608]{1,0:T(8,128)(2,1)}, f32[504,128]{1,0:T(8,128)}) custom-call(f32[192,4608]{1,0:T(8,128)S(1)} %get-tuple-element.8.acc, bf16[192,1280]{1,0:T(8,128)(2,1)S(1)} %get-tuple-element.9.pair, f32[288,256]{1,0:T(8,128)S(1)} %get-tuple-element.10.nm2, bf16[256,1024]{1,0:T(8,128)(2,1)S(1)} %get-tuple-element.11.diag), custom_call_target="tpu_custom_call" | custom-call | tf_op jit(solution)/shard_map/finish/pallas_call | solution.py:602
